TPU v7x, 32 devices: a whole 2x2x4 slice. The times are simulated.
32 devices in a mesh: flow: 8 (over y, x, core), chem: 4 (over z).
Axes of the slice: x: 2, y: 2, z: 4, core: 2. Of those that a mesh axis runs over, the one named last changes fastest.
Arguments:
- component_levels: float32 [512, 111, 512], P('flow', None, 'chem'), may hold values from 0.1 to 2
- thermal_field: float32 [512, 512], P('flow', 'chem'), may hold values from 0.5 to 2.7
- reciprocal_pair_diffusivity: float32 [111, 111], replicated, may hold values from 0.005 to 0.02
- log_arrhenius_factor: float32 [784], replicated, may hold values from -1 to 6
- kinetic_exponents: float32 [784, 111], replicated, may hold values from 0 to 0.05
- arrhenius_energies: float32 [784], replicated, may hold values from 0.5 to 4
- molar_change_matrix: float32 [111, 784], replicated, may hold values from -0.21875 to 0.21875
- cooling_by_component: float32 [111], replicated, may hold values from -1 to 1
- burning_flags: int32 [512, 4], P('flow', 'chem'), may hold values from 0 to 1, as said below
Outputs:
- advanced_components: float32 [512, 111, 512], P('flow', None, 'chem')
- advanced_thermal: float32 [512, 512], P('flow', 'chem')
Inputs may be any that keep to these rules, and one draw needn't show every extreme that they name: `burning_flags`: each device's 64 rows hold at most 24 reacting blocks, and at least one device of every chem index holds exactly 24; the devices of one chem index hold exactly 64 reacting blocks together.
All inputs are finite; a program needn't handle non-finite values.
Results may differ from a plain program's by a relative error of at most 0.000058.
Values sent between devices are 32-bit elements; how exact they have to be, the bound alone decides.
A program may use at most 192 MiB of HBM per device.

v0:
```python
from functools import partial
import math

import jax
import jax.numpy as jnp
from jax import lax
from jax.experimental import pallas as pl
from jax.experimental.pallas import tpu as pltpu
from jax.sharding import PartitionSpec as P

MESH = pl.DeviceIdType.MESH
F32 = jnp.float32
BF16 = jnp.bfloat16
courant = 0.2
chem_step = 0.05
log_offset = 0.001
rate_ceiling = 2.0
LOG2E = 1.0 / math.log(2.0)
CHUNK = 8
GROUP = 2


def split(x):
    hi = x.astype(BF16)
    return hi, (x - hi.astype(F32)).astype(BF16)


def flux_kernel(
    flow_n, chem_n, c_hbm, t_ref, rr_ref, f_hbm, dt_ref,
    cv, cx, dx, fv, col_out, col_in, peak, in_sem, out_sem, halo_send, halo_recv, max_send, max_recv,
):
    rows, species, lanes = cv.shape
    padded = cx.shape[1]
    chunks = rows // CHUNK
    fi, ci = lax.axis_index("flow"), lax.axis_index("chem")

    def chunk_in(k):
        at = pl.ds(k * CHUNK, CHUNK)
        return pltpu.make_async_copy(c_hbm.at[at], cv.at[at], in_sem.at[k])

    def chunk_out(k):
        at = pl.ds(k * CHUNK, CHUNK)
        return pltpu.make_async_copy(fv.at[at], f_hbm.at[at], out_sem.at[k])

    @pl.loop(0, chunks)
    def _(k):
        chunk_in(k).start()

    barrier = pltpu.get_barrier_semaphore()
    for k in range(1, flow_n):
        pl.semaphore_signal(barrier, inc=1, device_id=(lax.rem(fi + k, flow_n), ci), device_id_type=MESH)
    for k in range(1, chem_n):
        pl.semaphore_signal(barrier, inc=1, device_id=(fi, lax.rem(ci + k, chem_n)), device_id_type=MESH)

    lane = lax.broadcasted_iota(jnp.int32, (padded, lanes), 1)
    ones = jnp.ones((padded, lanes), F32)

    def prepare(x, cols):
        heads, tails = cols

        @pl.when(lax.rem(x, CHUNK) == 0)
        def _():
            chunk_in(x // CHUNK).wait()

        cx[x + 1, 0:species, :] = cv[x]
        cx[x + 1, species : species + 1, :] = t_ref[pl.ds(x, 1), :]
        row = cx[x + 1]
        head_at = lax.rem(2 * x + lanes - 1, lanes)
        heads = jnp.where(lane == head_at, pltpu.roll(row, head_at, 1), heads)
        tails = jnp.where(lane == 2 * x, pltpu.roll(row, lax.rem(2 * x + 1, lanes), 1), tails)
        return heads, tails

    heads, tails = lax.fori_loop(0, rows, prepare, (ones, ones))
    col_out[0] = heads
    col_out[1] = tails
    pl.semaphore_wait(barrier, flow_n + chem_n - 2)

    before, after = lax.rem(fi + flow_n - 1, flow_n), lax.rem(fi + 1, flow_n)
    west, east = lax.rem(ci + chem_n - 1, chem_n), lax.rem(ci + 1, chem_n)

    def halo(k, src, dst, device):
        return pltpu.make_async_remote_copy(
            src_ref=src, dst_ref=dst, send_sem=halo_send.at[k], recv_sem=halo_recv.at[k],
            device_id=device, device_id_type=MESH,
        )

    halos = [
        halo(0, cx.at[1], cx.at[rows + 1], (before, ci)),
        halo(1, cx.at[rows], cx.at[0], (after, ci)),
        halo(2, col_out.at[0], col_in.at[1], (fi, west)),
        halo(3, col_out.at[1], col_in.at[0], (fi, east)),
    ]
    for copy in halos:
        copy.start()

    def spreading(block):
        hi, lo = split(block)
        total = jnp.dot(rr_ref[...], jnp.concatenate([hi, lo], axis=0), preferred_element_type=F32)
        heat = block[species : species + 1, :]
        return heat * jnp.sqrt(heat) / (total[:padded] + total[padded:])

    def pair(p, top):
        d = spreading(jnp.concatenate([cx[2 * p + 1], cx[2 * p + 2]], axis=1))
        dx[2 * p + 1] = d[:, :lanes]
        dx[2 * p + 2] = d[:, lanes:]
        m = jnp.maximum(d[:, :lanes], d[:, lanes:])
        for s in range(0, padded, 8):
            top = jnp.maximum(top, m[s : s + 8])
        return top

    peak[0] = lax.fori_loop(0, rows // 2, pair, jnp.zeros((8, lanes), F32))

    def spread_max(base, count, who):
        return [
            pltpu.make_async_remote_copy(
                src_ref=peak.at[base], dst_ref=peak.at[base + k],
                send_sem=max_send.at[base + k], recv_sem=max_recv.at[base + k],
                device_id=who(k), device_id_type=MESH,
            )
            for k in range(1, count)
        ]

    first = spread_max(0, flow_n, lambda k: (lax.rem(fi + k, flow_n), ci))
    for copy in first:
        copy.start()

    for copy in halos:
        copy.wait()
    zero = jnp.zeros((padded, lanes), F32)
    d = spreading(jnp.concatenate([cx[0], cx[rows + 1]], axis=1))
    dx[0] = jnp.where(fi == 0, zero, d[:, :lanes])
    dx[rows + 1] = jnp.where(fi == flow_n - 1, zero, d[:, lanes:])
    cx[0] = jnp.where(fi == 0, zero, cx[0])
    cx[rows + 1] = jnp.where(fi == flow_n - 1, zero, cx[rows + 1])
    side = jnp.where(lax.rem(lane, 2) == 0, col_in[0], col_in[1])
    d = spreading(side)
    outside = (lax.rem(lane, 2) == 0) & (ci == 0) | (lax.rem(lane, 2) == 1) & (ci == chem_n - 1)
    col_in[0] = jnp.where(outside, zero, side)
    col_in[1] = jnp.where(outside, zero, d)

    def flux_row(x, above):
        c0, d0 = cx[x + 1], dx[x + 1]
        below = (dx[x + 2] + d0) * (cx[x + 2] - c0)
        turn = lax.rem(lanes - 2 * x, lanes)
        side_c = pltpu.roll(col_in[0], turn, 1)
        side_d = pltpu.roll(col_in[1], turn, 1)
        left_c = jnp.where(lane == 0, side_c, pltpu.roll(c0, 1, 1))
        left_d = jnp.where(lane == 0, side_d, pltpu.roll(d0, 1, 1))
        left = (left_d + d0) * (c0 - left_c)
        right = jnp.where(lane == lanes - 1, (side_d + d0) * (side_c - c0), pltpu.roll(left, lanes - 1, 1))
        fv[x] = 0.5 * ((below - above) + (right - left))
        return below

    def flux_chunk(k, above):
        for j in range(CHUNK):
            above = flux_row(k * CHUNK + j, above)
        chunk_out(k).start()
        return above

    above = (dx[0] + dx[1]) * (cx[1] - cx[0])
    above = lax.fori_loop(0, chunks // 2, flux_chunk, above)

    for copy in first:
        copy.wait()
    top = peak[0]
    for k in range(1, flow_n):
        top = jnp.maximum(top, peak[k])
    peak[flow_n] = top
    second = spread_max(flow_n, chem_n, lambda k: (fi, lax.rem(ci + k, chem_n)))
    for copy in second:
        copy.start()
    lax.fori_loop(chunks // 2, chunks, flux_chunk, above)
    for copy in second:
        copy.wait()
    for k in range(1, chem_n):
        top = jnp.maximum(top, peak[flow_n + k])
    dt_ref[...] = courant / jnp.broadcast_to(jnp.max(jnp.max(top, axis=1, keepdims=True), axis=0, keepdims=True), dt_ref.shape)

    @pl.loop(0, chunks)
    def _(k):
        chunk_out(k).wait()


def burn_kernel(
    flag_ref, c_hbm, f_hbm, t_ref, dt_ref, k_ref, m_ref, o_hbm, to_ref,
    cv, fv, xs, base, rate, place, c_sem, f_sem, o_sem,
):
    rows, species, lanes = cv.shape
    padded = fv.shape[1]
    chunks = rows // CHUNK
    width = GROUP * lanes

    def chunk_c(k):
        at = pl.ds(k * CHUNK, CHUNK)
        return pltpu.make_async_copy(c_hbm.at[at], cv.at[at], c_sem.at[k])

    def chunk_f(k):
        at = pl.ds(k * CHUNK, CHUNK)
        return pltpu.make_async_copy(f_hbm.at[at], fv.at[at], f_sem.at[k])

    def row_out(x):
        return pltpu.make_async_copy(cv.at[x], o_hbm.at[x], o_sem)

    @pl.loop(0, chunks)
    def _(k):
        chunk_c(k).start()
        chunk_f(k).start()

    to_ref[...] = t_ref[...]

    def listed(x, count):
        place[count] = x
        return count + flag_ref[x, 0]

    count = lax.fori_loop(0, rows, listed, jnp.int32(0))
    last = place[jnp.maximum(count - 1, 0)]
    for j in range(GROUP):
        place[count + j] = last

    step = dt_ref[0:1, :]

    @pl.loop(0, chunks)
    def _(k):
        chunk_c(k).wait()
        chunk_f(k).wait()
        for j in range(CHUNK):
            x = k * CHUNK + j
            cv[x] = cv[x] + step * fv[x, 0:species, :]

            @pl.when(flag_ref[x, 0] == 0)
            def _():
                row_out(x).start()

    row = lax.broadcasted_iota(jnp.int32, (padded, width), 0)
    extra = lax.broadcasted_iota(jnp.int32, (k_ref.shape[1] // 2 - padded, width), 0)
    ceiling = rate_ceiling * LOG2E

    @pl.loop(0, (count + GROUP - 1) // GROUP)
    def _(g):
        for j in range(GROUP):
            x = place[g * GROUP + j]
            at = slice(j * lanes, (j + 1) * lanes)
            xs[0:species, at] = cv[x]
            xs[species : species + 1, at] = t_ref[pl.ds(x, 1), :]
        x0 = xs[...]
        log1 = jnp.log(jnp.abs(x0) + log_offset)
        inverse = 1.0 / x0[species : species + 1, :]
        full = jnp.concatenate(
            [jnp.where(row == species, 1.0, log1), jnp.where(extra == 0, inverse, 0.0)], axis=0
        )
        hi, lo = split(full)
        terms = jnp.concatenate(
            [jnp.concatenate([hi, hi], axis=0), jnp.concatenate([lo, lo], axis=0)], axis=1
        )
        both = jnp.dot(k_ref[...], terms, preferred_element_type=F32)
        level = both[:, :width] + both[:, width:]
        base[...] = level
        r = jnp.exp2(jnp.minimum(level, ceiling))
        rate[...] = r
        hi, lo = split(r)
        wide = jnp.dot(m_ref[...], hi, preferred_element_type=F32)
        first = wide[:padded] + wide[padded:] + jnp.dot(m_ref[0:padded, :], lo, preferred_element_type=F32)

        def later(state):
            change = jnp.where(row == species, 0.0, jnp.log(jnp.abs(state) + log_offset) - log1)
            change = jnp.concatenate([change, jnp.zeros(extra.shape, F32)], axis=0).astype(BF16)
            level = base[...] + jnp.dot(
                k_ref[:, 0 : k_ref.shape[1] // 2], change, preferred_element_type=F32
            )
            r = jnp.exp2(jnp.minimum(level, ceiling))
            return first + jnp.dot(
                m_ref[0:padded, :], (r - rate[...]).astype(BF16), preferred_element_type=F32
            )

        second = later(x0 + (0.5 * chem_step) * first)
        total = first + 2.0 * second
        third = later(x0 + (0.5 * chem_step) * second)
        total = total + 2.0 * third
        total = total + later(x0 + chem_step * third)
        xs[...] = x0 + (chem_step / 6.0) * total
        for j in range(GROUP):
            x = place[g * GROUP + j]
            at = slice(j * lanes, (j + 1) * lanes)

            @pl.when(g * GROUP + j < count)
            def _():
                cv[x] = xs[0:species, at]
                to_ref[pl.ds(x, 1), :] = xs[species : species + 1, at]
                row_out(x).start()

    pltpu.make_async_copy(cv, o_hbm, o_sem).wait()


def halves(x):
    hi = lax.reduce_precision(x, 8, 7)
    return hi.astype(BF16), (x - hi).astype(BF16)


def per_device(
    flow_n, chem_n,
    component_levels, thermal_field, reciprocal_pair_diffusivity, log_arrhenius_factor,
    kinetic_exponents, arrhenius_energies, molar_change_matrix, cooling_by_component, burning_flags,
):
    rows, species, lanes = component_levels.shape
    reactions = kinetic_exponents.shape[0]
    padded = (species + 16) // 16 * 16
    depth = (padded + 1 + 127) // 128 * 128
    chunks = rows // CHUNK

    pairs = jnp.pad(reciprocal_pair_diffusivity, ((0, padded - species), (0, 0)), constant_values=1.0)
    pairs = jnp.pad(pairs, ((0, 0), (0, padded - species)))
    hi, lo = halves(pairs)
    pairs = jnp.concatenate([jnp.concatenate([hi, hi], 1), jnp.concatenate([lo, lo], 1)], 0)

    orders = jnp.concatenate(
        [
            kinetic_exponents,
            log_arrhenius_factor[:, None],
            jnp.zeros((reactions, padded - species - 1), F32),
            -arrhenius_energies[:, None],
            jnp.zeros((reactions, depth - padded - 1), F32),
        ],
        axis=1,
    ) * LOG2E
    orders = jnp.concatenate(halves(orders), axis=1)

    cooling = jnp.dot(cooling_by_component, molar_change_matrix, precision=lax.Precision.HIGHEST)
    changes = jnp.concatenate(
        [molar_change_matrix, -cooling[None], jnp.zeros((padded - species - 1, reactions), F32)], axis=0
    )
    changes = jnp.concatenate(halves(changes), axis=0)

    vmem = pl.BlockSpec(memory_space=pltpu.VMEM)
    smem = pl.BlockSpec(memory_space=pltpu.SMEM)
    anywhere = pl.BlockSpec(memory_space=pl.ANY)
    flux, step = pl.pallas_call(
        partial(flux_kernel, flow_n, chem_n),
        out_shape=(
            jax.ShapeDtypeStruct((rows, padded, lanes), F32),
            jax.ShapeDtypeStruct((8, lanes), F32),
        ),
        in_specs=[anywhere, vmem, vmem],
        out_specs=(anywhere, vmem),
        scratch_shapes=[
            pltpu.VMEM((rows, species, lanes), F32),
            pltpu.VMEM((rows + 2, padded, lanes), F32),
            pltpu.VMEM((rows + 2, padded, lanes), F32),
            pltpu.VMEM((rows, padded, lanes), F32),
            pltpu.VMEM((2, padded, lanes), F32),
            pltpu.VMEM((2, padded, lanes), F32),
            pltpu.VMEM((flow_n + chem_n, 8, lanes), F32),
            pltpu.SemaphoreType.DMA((chunks,)),
            pltpu.SemaphoreType.DMA((chunks,)),
            pltpu.SemaphoreType.DMA((4,)),
            pltpu.SemaphoreType.DMA((4,)),
            pltpu.SemaphoreType.DMA((flow_n + chem_n,)),
            pltpu.SemaphoreType.DMA((flow_n + chem_n,)),
        ],
        compiler_params=pltpu.CompilerParams(
            collective_id=0, has_side_effects=True, vmem_limit_bytes=40 * 2**20
        ),
        name="flux",
    )(component_levels, thermal_field, pairs)

    return pl.pallas_call(
        burn_kernel,
        out_shape=(
            jax.ShapeDtypeStruct((rows, species, lanes), F32),
            jax.ShapeDtypeStruct((rows, lanes), F32),
        ),
        in_specs=[smem, anywhere, anywhere, vmem, vmem, vmem, vmem],
        out_specs=(anywhere, vmem),
        scratch_shapes=[
            pltpu.VMEM((rows, species, lanes), F32),
            pltpu.VMEM((rows, padded, lanes), F32),
            pltpu.VMEM((padded, GROUP * lanes), F32),
            pltpu.VMEM((reactions, GROUP * lanes), F32),
            pltpu.VMEM((reactions, GROUP * lanes), F32),
            pltpu.SMEM((rows + GROUP,), jnp.int32),
            pltpu.SemaphoreType.DMA((chunks,)),
            pltpu.SemaphoreType.DMA((chunks,)),
            pltpu.SemaphoreType.DMA(()),
        ],
        compiler_params=pltpu.CompilerParams(vmem_limit_bytes=48 * 2**20),
        name="burn",
    )(burning_flags, component_levels, flux, thermal_field, step, orders, changes)


def solution(mesh):
    placed = (
        P("flow", None, "chem"),
        P("flow", "chem"),
        P(),
        P(),
        P(),
        P(),
        P(),
        P(),
        P("flow", "chem"),
    )
    return jax.shard_map(
        partial(per_device, mesh.shape["flow"], mesh.shape["chem"]),
        mesh=mesh,
        in_specs=placed,
        out_specs=(P("flow", None, "chem"), P("flow", "chem")),
        check_vma=False,
    )
```

profile of v0, /device:TPU:21, one launch (start us, length us, event | category | flops | bytes accessed | tf_op | source)
XLA Modules:
  0.0 79.2 jit_solution(4784133879943867015)
XLA Ops:
  0.6 0.0 copy-start
  0.7 0.1 pad.19.clone
  0.7 0.7 neg.12
  1.4 0.0 copy-done
  1.4 1.3 %convolution_reduce_fusion = f32[784]{0:T(1024)S(1)} fusion(f32[111,784]{1,0:T(8,128)} %param.15, f32[111]{0:T(128)S(1)} %copy-done), kind=kOutput, calls=%fused_computation | convolution fusion | flops 1044288 | bytes 351676 | tf_op jit(solution)/shard_map/dot_general | solution.py:327
  2.8 0.7 copy.18.flag_ref
  3.5 0.0 copy-start.4
  3.5 1.0 %reduce-precision_convert_fusion.2 = (bf16[112,112]{1,0:T(8,128)(2,1)S(1)}, bf16[112,112]{1,0:T(8,128)(2,1)S(1)}) fusion(f32[111,111]{1,0:T(8,128)} %param.11), kind=kLoop, calls=%fused_computation.13 | loop fusion | flops 75264 | bytes 99460 | tf_op jit(solution)/shard_map/convert_element_type | solution.py:296
  4.5 0.1 maximum_maximum_fusion.rr_ref
  4.6 0.2 neg.16
  4.8 1.1 %reduce-precision_convert_fusion = (bf16[112,784]{1,0:T(8,128)(2,1)S(1)}, bf16[112,784]{1,0:T(8,128)(2,1)S(1)}) fusion(f32[1,784]{1,0:T(1,128)S(1)} %neg.15, f32[111,784]{1,0:T(8,128)} %param.15), kind=kLoop, calls=%fused_computation.2 | loop fusion | flops 439040 | bytes 702464 | tf_op jit(solution)/shard_map/convert_element_type | solution.py:296
  5.9 0.8 %broadcast_in_dim.10 = f32[784,1]{1,0:T(8,128)S(1)} reshape(f32[784]{0:T(1024)} %param.12) | data formatting | bytes 6272 | tf_op jit(solution)/shard_map/broadcast_in_dim | solution.py:318
  6.8 1.3 %reduce-precision_convert_fusion.1 = (bf16[784,128]{1,0:T(8,128)(2,1)S(1)}, f32[784,128]{1,0:T(8,128)S(1)}) fusion(f32[128]{0:T(128)S(1)} %pad.19.clone, f32[784,1]{1,0:T(8,128)S(1)} %neg.16, f32[784,1]{1,0:T(8,128)S(1)} %broadcast_in_dim.10, f32[784,111]{1,0:T(8,128)} %param.13), kind=kLoop, calls=%fused_computation.4 | loop fusion | flops 602112 | bytes 956992 | tf_op jit(solution)/shard_map/convert_element_type | solution.py:296
  8.2 0.0 copy-done.4
  8.2 0.0 copy-start.3
  8.2 2.1 %copy.19.c_hbm = f32[64,111,128]{2,1,0:T(8,128)S(1)} copy(f32[64,111,128]{2,0,1:T(8,128)S(1)} %copy-done.4) | data formatting | bytes 7274496 | tf_op args[0]
  10.3 0.0 copy-done.3
  10.3 0.0 copy-start.1
  10.3 25.2 %flux.1 = (f32[64,112,128]{2,1,0:T(8,128)S(1)}, f32[8,128]{1,0:T(8,128)S(1)}) custom-call(f32[64,111,128]{2,1,0:T(8,128)S(1)} %copy.19.c_hbm, f32[64,128]{1,0:T(8,128)S(1)} %copy-done.3, bf16[224,224]{1,0:T(8,128)(2,1)S(1)} %maximum_maximum_fusion.rr_ref), custom_call_target="tpu_custom_call" | custom-call | tf_op jit(solution)/shard_map/flux/pallas_call | solution.py:336
  35.5 0.0 copy-start.2
  35.5 1.8 %copy-done.2 = f32[64,112,128]{2,1,0:T(8,128)} copy-done((f32[64,112,128]{2,1,0:T(8,128)}, f32[64,112,128]{2,1,0:T(8,128)S(1)}, u32[]{:S(2)}) %copy-start.2) | copy-done | bytes 3670040
  37.4 0.0 copy-done.1
  37.4 38.9 %burn.1 = (f32[64,111,128]{2,1,0:T(8,128)S(1)}, f32[64,128]{1,0:T(8,128)}) custom-call(s32[64,1]{1,0:T(8,128)S(1)} %copy.18.flag_ref, f32[64,111,128]{2,1,0:T(8,128)} %copy-done.1, f32[64,112,128]{2,1,0:T(8,128)} %copy-done.2, f32[64,128]{1,0:T(8,128)S(1)} %copy-done.3, f32[8,128]{1,0:T(8,128)S(1)} %get-tuple-element.5.dt_ref, ...), custom_call_target="tpu_custom_call" | custom-call | tf_op jit(solution)/shard_map/burn/pallas_call | solution.py:365
  76.2 2.9 %copy.20 = f32[64,111,128]{2,0,1:T(8,128)} copy(f32[64,111,128]{2,1,0:T(8,128)S(1)} %get-tuple-element.8) | data formatting | bytes 7274496 | tf_op jit(solution)/shard_map/burn/pallas_call | solution.py:365
  (6 shorter events, 0.1 us)
Async XLA Ops:
  0.6 0.8 %copy-start = (f32[111]{0:T(128)S(1)}, f32[111]{0:T(128)}, u32[]{:S(2)}) copy-start(f32[111]{0:T(128)} %param.16) | copy-start | bytes 1336
  3.5 4.6 %copy-start.4 = (f32[64,111,128]{2,0,1:T(8,128)S(1)}, f32[64,111,128]{2,0,1:T(8,128)}, u32[]{:S(2)}) copy-start(f32[64,111,128]{2,0,1:T(8,128)} %param.9) | copy-start | bytes 10911748
  8.2 2.1 %copy-start.3 = (f32[64,128]{1,0:T(8,128)S(1)}, f32[64,128]{1,0:T(8,128)}, u32[]{:S(2)}) copy-start(f32[64,128]{1,0:T(8,128)} %t_ref.3) | copy-start | bytes 98308
  10.3 27.1 %copy-start.1 = (f32[64,111,128]{2,1,0:T(8,128)}, f32[64,111,128]{2,1,0:T(8,128)S(1)}, u32[]{:S(2)}) copy-start(f32[64,111,128]{2,1,0:T(8,128)S(1)} %copy.19.c_hbm) | copy-start | bytes 10911748
  35.5 1.8 %copy-start.2 = (f32[64,112,128]{2,1,0:T(8,128)}, f32[64,112,128]{2,1,0:T(8,128)S(1)}, u32[]{:S(2)}) copy-start(f32[64,112,128]{2,1,0:T(8,128)S(1)} %get-tuple-element.4.f_hbm) | copy-start | bytes 11010052
where the time goes:
time: 80.7 us; the launch traced here: 79.2 us
  Pallas kernels  64.1 us (79%)
  local copies, waits for them, and re-layouts  8.73 us (11%)
  other arithmetic  4.26 us (5%)
  matrix products  1.32 us (2%)
    pallas_call x1, Pallas kernels, per_device(): pl.pallas_call(burn_kernel, out_shape=(jax.ShapeDtypeStruct((rows, specie...  38.9 us
    pallas_call x1, Pallas kernels, per_device(): pl.pallas_call(partial(flux_kernel, flow_n, chem_n), out_shape=(jax.Shape...  25.2 us
    unnamed x12, local copies, waits for them, and re-layouts  4.7 us
    convert_element_type x4, other arithmetic, halves(): return (hi.astype(BF16), (x - hi).astype(BF16))  3.38 us
    pallas_call x1, local copies, waits for them, and re-layouts, per_device(): pl.pallas_call(burn_kernel, out_shape=(jax.ShapeDtypeStruct((rows, specie...  2.94 us

commit v1 on v0

--- a/solution.py
+++ b/solution.py
@@ -17,7 +17,8 @@
 rate_ceiling = 2.0
 LOG2E = 1.0 / math.log(2.0)
 CHUNK = 8
-GROUP = 2
+GROUP = 4
+VMEM_BYTES = 56 * 2**20
 
 
 def split(x):
@@ -25,18 +26,26 @@
     return hi, (x - hi.astype(F32)).astype(BF16)
 
 
+def row_copies(start, k, species_hbm, rows_vmem, sem):
+    for j in range(CHUNK):
+        x = k * CHUNK + j
+        copy = pltpu.make_async_copy(species_hbm.at[:, x], rows_vmem.at[x], sem.at[x])
+        if start:
+            copy.start()
+        else:
+            copy.wait()
+
+
 def flux_kernel(
-    flow_n, chem_n, c_hbm, t_ref, rr_ref, f_hbm, dt_ref,
-    cv, cx, dx, fv, col_out, col_in, peak, in_sem, out_sem, halo_send, halo_recv, max_send, max_recv,
+    flow_n, chem_n, c_hbm, t_ref, pair_ref, f_hbm, dt_ref,
+    cv, cx, dx, fv, pairs, rr_ref, col_out, col_in, peak,
+    in_sem, out_sem, halo_send, halo_recv, max_send, max_recv,
 ):
     rows, species, lanes = cv.shape
     padded = cx.shape[1]
+    depth = pairs.shape[1]
     chunks = rows // CHUNK
     fi, ci = lax.axis_index("flow"), lax.axis_index("chem")
-
-    def chunk_in(k):
-        at = pl.ds(k * CHUNK, CHUNK)
-        return pltpu.make_async_copy(c_hbm.at[at], cv.at[at], in_sem.at[k])
 
     def chunk_out(k):
         at = pl.ds(k * CHUNK, CHUNK)
@@ -44,7 +53,7 @@
 
     @pl.loop(0, chunks)
     def _(k):
-        chunk_in(k).start()
+        row_copies(True, k, c_hbm, cv, in_sem)
 
     barrier = pltpu.get_barrier_semaphore()
     for k in range(1, flow_n):
@@ -52,25 +61,33 @@
     for k in range(1, chem_n):
         pl.semaphore_signal(barrier, inc=1, device_id=(fi, lax.rem(ci + k, chem_n)), device_id_type=MESH)
 
+    at_col = lax.broadcasted_iota(jnp.int32, pairs.shape, 1)
+    pairs[...] = jnp.where(at_col < species, 1.0, 0.0)
+    pairs[0:species, 0:species] = pair_ref[...]
+    hi, lo = split(pairs[...])
+    rr_ref[...] = jnp.concatenate(
+        [jnp.concatenate([hi, hi], axis=1), jnp.concatenate([lo, lo], axis=1)], axis=0
+    )
+
     lane = lax.broadcasted_iota(jnp.int32, (padded, lanes), 1)
     ones = jnp.ones((padded, lanes), F32)
 
-    def prepare(x, cols):
+    def prepare(k, cols):
         heads, tails = cols
-
-        @pl.when(lax.rem(x, CHUNK) == 0)
-        def _():
-            chunk_in(x // CHUNK).wait()
-
-        cx[x + 1, 0:species, :] = cv[x]
-        cx[x + 1, species : species + 1, :] = t_ref[pl.ds(x, 1), :]
-        row = cx[x + 1]
-        head_at = lax.rem(2 * x + lanes - 1, lanes)
-        heads = jnp.where(lane == head_at, pltpu.roll(row, head_at, 1), heads)
-        tails = jnp.where(lane == 2 * x, pltpu.roll(row, lax.rem(2 * x + 1, lanes), 1), tails)
+        row_copies(False, k, c_hbm, cv, in_sem)
+        for j in range(CHUNK):
+            x = k * CHUNK + j
+            cx[x + 1, 0:species, :] = cv[x]
+            cx[x + 1, species : species + 1, :] = t_ref[pl.ds(x, 1), :]
+        for j in range(CHUNK):
+            x = k * CHUNK + j
+            row = cx[x + 1]
+            head_at = lax.rem(2 * x + lanes - 1, lanes)
+            heads = jnp.where(lane == head_at, pltpu.roll(row, head_at, 1), heads)
+            tails = jnp.where(lane == 2 * x, pltpu.roll(row, lax.rem(2 * x + 1, lanes), 1), tails)
         return heads, tails
 
-    heads, tails = lax.fori_loop(0, rows, prepare, (ones, ones))
+    heads, tails = lax.fori_loop(0, chunks, prepare, (ones, ones))
     col_out[0] = heads
     col_out[1] = tails
     pl.semaphore_wait(barrier, flow_n + chem_n - 2)
@@ -95,20 +112,26 @@
 
     def spreading(block):
         hi, lo = split(block)
-        total = jnp.dot(rr_ref[...], jnp.concatenate([hi, lo], axis=0), preferred_element_type=F32)
+        blank = jnp.zeros((depth - padded, block.shape[1]), BF16)
+        total = jnp.dot(
+            rr_ref[...], jnp.concatenate([hi, blank, lo, blank], axis=0), preferred_element_type=F32
+        )
         heat = block[species : species + 1, :]
         return heat * jnp.sqrt(heat) / (total[:padded] + total[padded:])
 
-    def pair(p, top):
-        d = spreading(jnp.concatenate([cx[2 * p + 1], cx[2 * p + 2]], axis=1))
-        dx[2 * p + 1] = d[:, :lanes]
-        dx[2 * p + 2] = d[:, lanes:]
-        m = jnp.maximum(d[:, :lanes], d[:, lanes:])
+    def diffusivities(k, top):
+        first = k * CHUNK + 1
+        d = spreading(jnp.concatenate([cx[first + j] for j in range(CHUNK)], axis=1))
+        m = d[:, :lanes]
+        for j in range(CHUNK):
+            here = d[:, j * lanes : (j + 1) * lanes]
+            dx[first + j] = here
+            m = jnp.maximum(m, here)
         for s in range(0, padded, 8):
             top = jnp.maximum(top, m[s : s + 8])
         return top
 
-    peak[0] = lax.fori_loop(0, rows // 2, pair, jnp.zeros((8, lanes), F32))
+    peak[0] = lax.fori_loop(0, chunks, diffusivities, jnp.zeros((8, lanes), F32))
 
     def spread_max(base, count, who):
         return [
@@ -127,38 +150,42 @@
     for copy in halos:
         copy.wait()
     zero = jnp.zeros((padded, lanes), F32)
-    d = spreading(jnp.concatenate([cx[0], cx[rows + 1]], axis=1))
+    side = jnp.where(lax.rem(lane, 2) == 0, col_in[0], col_in[1])
+    d = spreading(jnp.concatenate([cx[0], cx[rows + 1], side], axis=1))
     dx[0] = jnp.where(fi == 0, zero, d[:, :lanes])
-    dx[rows + 1] = jnp.where(fi == flow_n - 1, zero, d[:, lanes:])
+    dx[rows + 1] = jnp.where(fi == flow_n - 1, zero, d[:, lanes : 2 * lanes])
     cx[0] = jnp.where(fi == 0, zero, cx[0])
     cx[rows + 1] = jnp.where(fi == flow_n - 1, zero, cx[rows + 1])
-    side = jnp.where(lax.rem(lane, 2) == 0, col_in[0], col_in[1])
-    d = spreading(side)
     outside = (lax.rem(lane, 2) == 0) & (ci == 0) | (lax.rem(lane, 2) == 1) & (ci == chem_n - 1)
     col_in[0] = jnp.where(outside, zero, side)
-    col_in[1] = jnp.where(outside, zero, d)
-
-    def flux_row(x, above):
-        c0, d0 = cx[x + 1], dx[x + 1]
-        below = (dx[x + 2] + d0) * (cx[x + 2] - c0)
-        turn = lax.rem(lanes - 2 * x, lanes)
-        side_c = pltpu.roll(col_in[0], turn, 1)
-        side_d = pltpu.roll(col_in[1], turn, 1)
-        left_c = jnp.where(lane == 0, side_c, pltpu.roll(c0, 1, 1))
-        left_d = jnp.where(lane == 0, side_d, pltpu.roll(d0, 1, 1))
-        left = (left_d + d0) * (c0 - left_c)
-        right = jnp.where(lane == lanes - 1, (side_d + d0) * (side_c - c0), pltpu.roll(left, lanes - 1, 1))
-        fv[x] = 0.5 * ((below - above) + (right - left))
-        return below
-
-    def flux_chunk(k, above):
-        for j in range(CHUNK):
-            above = flux_row(k * CHUNK + j, above)
+    col_in[1] = jnp.where(outside, zero, d[:, 2 * lanes :])
+
+    at_lane = lax.broadcasted_iota(jnp.int32, (8, lanes), 1)
+
+    def flux_chunk(k):
+        for s in range(0, padded, 8):
+            at = slice(s, s + 8)
+            x = k * CHUNK
+            c0, d0 = cx[x + 1, at, :], dx[x + 1, at, :]
+            above = (dx[x, at, :] + d0) * (c0 - cx[x, at, :])
+            for j in range(CHUNK):
+                x = k * CHUNK + j
+                c1, d1 = cx[x + 2, at, :], dx[x + 2, at, :]
+                below = (d1 + d0) * (c1 - c0)
+                turn = lax.rem(lanes - 2 * x, lanes)
+                side_c = pltpu.roll(col_in[0, at, :], turn, 1)
+                side_d = pltpu.roll(col_in[1, at, :], turn, 1)
+                left_c = jnp.where(at_lane == 0, side_c, pltpu.roll(c0, 1, 1))
+                left_d = jnp.where(at_lane == 0, side_d, pltpu.roll(d0, 1, 1))
+                left = (left_d + d0) * (c0 - left_c)
+                right = jnp.where(
+                    at_lane == lanes - 1, (side_d + d0) * (side_c - c0), pltpu.roll(left, lanes - 1, 1)
+                )
+                fv[x, at, :] = 0.5 * ((below - above) + (right - left))
+                c0, d0, above = c1, d1, below
         chunk_out(k).start()
-        return above
-
-    above = (dx[0] + dx[1]) * (cx[1] - cx[0])
-    above = lax.fori_loop(0, chunks // 2, flux_chunk, above)
+
+    pl.loop(0, chunks // 2)(flux_chunk)
 
     for copy in first:
         copy.wait()
@@ -169,12 +196,14 @@
     second = spread_max(flow_n, chem_n, lambda k: (fi, lax.rem(ci + k, chem_n)))
     for copy in second:
         copy.start()
-    lax.fori_loop(chunks // 2, chunks, flux_chunk, above)
+    pl.loop(chunks // 2, chunks)(flux_chunk)
     for copy in second:
         copy.wait()
     for k in range(1, chem_n):
         top = jnp.maximum(top, peak[flow_n + k])
-    dt_ref[...] = courant / jnp.broadcast_to(jnp.max(jnp.max(top, axis=1, keepdims=True), axis=0, keepdims=True), dt_ref.shape)
+    dt_ref[...] = courant / jnp.broadcast_to(
+        jnp.max(jnp.max(top, axis=1, keepdims=True), axis=0, keepdims=True), dt_ref.shape
+    )
 
     @pl.loop(0, chunks)
     def _(k):
@@ -182,52 +211,72 @@
 
 
 def burn_kernel(
-    flag_ref, c_hbm, f_hbm, t_ref, dt_ref, k_ref, m_ref, o_hbm, to_ref,
-    cv, fv, xs, base, rate, place, c_sem, f_sem, o_sem,
+    flag_ref, c_hbm, f_hbm, t_ref, dt_ref, factor_ref, order_ref, energy_ref, change_ref, cool_ref,
+    o_hbm, to_ref,
+    cv, fv, xs, base, rate, wide_k, side_k, wide_m, k_ref, m_ref, place, c_sem, f_sem, o_sem,
 ):
     rows, species, lanes = cv.shape
     padded = fv.shape[1]
+    depth = wide_k.shape[1]
+    reactions = wide_k.shape[0]
     chunks = rows // CHUNK
     width = GROUP * lanes
-
-    def chunk_c(k):
-        at = pl.ds(k * CHUNK, CHUNK)
-        return pltpu.make_async_copy(c_hbm.at[at], cv.at[at], c_sem.at[k])
 
     def chunk_f(k):
         at = pl.ds(k * CHUNK, CHUNK)
         return pltpu.make_async_copy(f_hbm.at[at], fv.at[at], f_sem.at[k])
 
     def row_out(x):
-        return pltpu.make_async_copy(cv.at[x], o_hbm.at[x], o_sem)
+        return pltpu.make_async_copy(cv.at[x], o_hbm.at[:, x], o_sem)
 
     @pl.loop(0, chunks)
     def _(k):
-        chunk_c(k).start()
+        row_copies(True, k, c_hbm, cv, c_sem)
         chunk_f(k).start()
 
     to_ref[...] = t_ref[...]
 
     def listed(x, count):
         place[count] = x
-        return count + flag_ref[x, 0]
+        return count + flag_ref[0, x]
 
     count = lax.fori_loop(0, rows, listed, jnp.int32(0))
     last = place[jnp.maximum(count - 1, 0)]
     for j in range(GROUP):
         place[count + j] = last
 
+    wide_k[...] = jnp.zeros(wide_k.shape, F32)
+    wide_k[:, 0:species] = order_ref[...]
+    side_k[...] = jnp.zeros(side_k.shape, F32)
+    side_k[species : species + 1, 0:reactions] = factor_ref[...]
+    side_k[padded : padded + 1, 0:reactions] = -energy_ref[...]
+    hi, lo = split((wide_k[...] + side_k[...].T[0:reactions, :]) * LOG2E)
+    k_ref[:, 0:depth] = hi
+    k_ref[:, depth:] = lo
+    cooled = jnp.dot(
+        jnp.broadcast_to(cool_ref[...], (8, species)), change_ref[...],
+        precision=lax.Precision.HIGHEST, preferred_element_type=F32,
+    )
+    wide_m[...] = jnp.zeros(wide_m.shape, F32)
+    wide_m[0:species, :] = change_ref[...]
+    wide_m[species : species + 1, :] = -cooled[0:1]
+    hi, lo = split(wide_m[...])
+    m_ref[0:padded, :] = hi
+    m_ref[padded:, :] = lo
+
     step = dt_ref[0:1, :]
 
     @pl.loop(0, chunks)
     def _(k):
-        chunk_c(k).wait()
+        row_copies(False, k, c_hbm, cv, c_sem)
         chunk_f(k).wait()
         for j in range(CHUNK):
             x = k * CHUNK + j
             cv[x] = cv[x] + step * fv[x, 0:species, :]
-
-            @pl.when(flag_ref[x, 0] == 0)
+        for j in range(CHUNK):
+            x = k * CHUNK + j
+
+            @pl.when(flag_ref[0, x] == 0)
             def _():
                 row_out(x).start()
 
@@ -288,12 +337,9 @@
                 to_ref[pl.ds(x, 1), :] = xs[species : species + 1, at]
                 row_out(x).start()
 
-    pltpu.make_async_copy(cv, o_hbm, o_sem).wait()
-
-
-def halves(x):
-    hi = lax.reduce_precision(x, 8, 7)
-    return hi.astype(BF16), (x - hi).astype(BF16)
+    @pl.loop(0, rows)
+    def _(x):
+        row_out(x).wait()
 
 
 def per_device(
@@ -307,29 +353,7 @@
     depth = (padded + 1 + 127) // 128 * 128
     chunks = rows // CHUNK
 
-    pairs = jnp.pad(reciprocal_pair_diffusivity, ((0, padded - species), (0, 0)), constant_values=1.0)
-    pairs = jnp.pad(pairs, ((0, 0), (0, padded - species)))
-    hi, lo = halves(pairs)
-    pairs = jnp.concatenate([jnp.concatenate([hi, hi], 1), jnp.concatenate([lo, lo], 1)], 0)
-
-    orders = jnp.concatenate(
-        [
-            kinetic_exponents,
-            log_arrhenius_factor[:, None],
-            jnp.zeros((reactions, padded - species - 1), F32),
-            -arrhenius_energies[:, None],
-            jnp.zeros((reactions, depth - padded - 1), F32),
-        ],
-        axis=1,
-    ) * LOG2E
-    orders = jnp.concatenate(halves(orders), axis=1)
-
-    cooling = jnp.dot(cooling_by_component, molar_change_matrix, precision=lax.Precision.HIGHEST)
-    changes = jnp.concatenate(
-        [molar_change_matrix, -cooling[None], jnp.zeros((padded - species - 1, reactions), F32)], axis=0
-    )
-    changes = jnp.concatenate(halves(changes), axis=0)
-
+    levels = component_levels.transpose(1, 0, 2)
     vmem = pl.BlockSpec(memory_space=pltpu.VMEM)
     smem = pl.BlockSpec(memory_space=pltpu.SMEM)
     anywhere = pl.BlockSpec(memory_space=pl.ANY)
@@ -346,10 +370,12 @@
             pltpu.VMEM((rows + 2, padded, lanes), F32),
             pltpu.VMEM((rows + 2, padded, lanes), F32),
             pltpu.VMEM((rows, padded, lanes), F32),
+            pltpu.VMEM((padded, depth), F32),
+            pltpu.VMEM((2 * padded, 2 * depth), BF16),
             pltpu.VMEM((2, padded, lanes), F32),
             pltpu.VMEM((2, padded, lanes), F32),
             pltpu.VMEM((flow_n + chem_n, 8, lanes), F32),
-            pltpu.SemaphoreType.DMA((chunks,)),
+            pltpu.SemaphoreType.DMA((rows,)),
             pltpu.SemaphoreType.DMA((chunks,)),
             pltpu.SemaphoreType.DMA((4,)),
             pltpu.SemaphoreType.DMA((4,)),
@@ -357,18 +383,18 @@
             pltpu.SemaphoreType.DMA((flow_n + chem_n,)),
         ],
         compiler_params=pltpu.CompilerParams(
-            collective_id=0, has_side_effects=True, vmem_limit_bytes=40 * 2**20
+            collective_id=0, has_side_effects=True, vmem_limit_bytes=VMEM_BYTES
         ),
         name="flux",
-    )(component_levels, thermal_field, pairs)
-
-    return pl.pallas_call(
+    )(levels, thermal_field, reciprocal_pair_diffusivity)
+
+    advanced, heat = pl.pallas_call(
         burn_kernel,
         out_shape=(
-            jax.ShapeDtypeStruct((rows, species, lanes), F32),
+            jax.ShapeDtypeStruct((species, rows, lanes), F32),
             jax.ShapeDtypeStruct((rows, lanes), F32),
         ),
-        in_specs=[smem, anywhere, anywhere, vmem, vmem, vmem, vmem],
+        in_specs=[smem, anywhere, anywhere] + [vmem] * 7,
         out_specs=(anywhere, vmem),
         scratch_shapes=[
             pltpu.VMEM((rows, species, lanes), F32),
@@ -376,14 +402,23 @@
             pltpu.VMEM((padded, GROUP * lanes), F32),
             pltpu.VMEM((reactions, GROUP * lanes), F32),
             pltpu.VMEM((reactions, GROUP * lanes), F32),
+            pltpu.VMEM((reactions, depth), F32),
+            pltpu.VMEM((depth, (reactions + 127) // 128 * 128), F32),
+            pltpu.VMEM((padded, reactions), F32),
+            pltpu.VMEM((reactions, 2 * depth), BF16),
+            pltpu.VMEM((2 * padded, reactions), BF16),
             pltpu.SMEM((rows + GROUP,), jnp.int32),
-            pltpu.SemaphoreType.DMA((chunks,)),
+            pltpu.SemaphoreType.DMA((rows,)),
             pltpu.SemaphoreType.DMA((chunks,)),
             pltpu.SemaphoreType.DMA(()),
         ],
-        compiler_params=pltpu.CompilerParams(vmem_limit_bytes=48 * 2**20),
+        compiler_params=pltpu.CompilerParams(vmem_limit_bytes=VMEM_BYTES),
         name="burn",
-    )(burning_flags, component_levels, flux, thermal_field, step, orders, changes)
+    )(
+        burning_flags.T, levels, flux, thermal_field, step, log_arrhenius_factor[None],
+        kinetic_exponents, arrhenius_energies[None], molar_change_matrix, cooling_by_component[None],
+    )
+    return advanced.transpose(1, 0, 2), heat
 
 
 def solution(mesh):

time: 80.7 us -> 94 us (1.16)
  the two profiles are of different devices: /device:TPU:21 before, /device:TPU:6 now
where the time goes in v1:
time: 94 us; the launch traced here: 93.8 us
  Pallas kernels  90.6 us (96%)
  local copies, waits for them, and re-layouts  2.55 us (3%)
    pallas_call x1, Pallas kernels, per_device(): pl.pallas_call(partial(flux_kernel, flow_n, chem_n), out_shape=(jax.Shape...  65.2 us
    pallas_call x1, Pallas kernels, per_device(): pl.pallas_call(burn_kernel, out_shape=(jax.ShapeDtypeStruct((species, row...  25.4 us

profile of v1, /device:TPU:6, one launch (start us, length us, event | category | flops | bytes accessed | tf_op | source)
XLA Modules:
  0.0 93.8 jit_solution(13493453230166002853)
XLA Ops:
  0.6 1.3 %broadcast_in_dim.9.factor_ref = f32[1,784]{1,0:T(1,128)} reshape(f32[784]{0:T(1024)} %param.12) | data formatting | bytes 6272 | tf_op jit(solution)/shard_map/broadcast_in_dim | solution.py:418
  1.9 1.3 %broadcast_in_dim.10.energy_ref = f32[1,784]{1,0:T(1,128)} reshape(f32[784]{0:T(1024)} %param.14) | data formatting | bytes 6272 | tf_op jit(solution)/shard_map/broadcast_in_dim | solution.py:419
  3.2 65.2 %flux.1 = (f32[64,112,128]{2,1,0:T(8,128)}, f32[8,128]{1,0:T(8,128)}) custom-call(f32[111,64,128]{2,1,0:T(8,128)} %bitcast.4, f32[64,128]{1,0:T(8,128)} %t_ref.3, f32[111,111]{1,0:T(8,128)} %pair_ref.1), custom_call_target="tpu_custom_call" | custom-call | tf_op jit(solution)/shard_map/flux/pallas_call | solution.py:360
  68.4 25.4 %burn.1 = (f32[111,64,128]{2,1,0:T(8,128)}, f32[64,128]{1,0:T(8,128)}) custom-call(s32[1,64]{1,0:T(1,128)} %bitcast.6, f32[111,64,128]{2,1,0:T(8,128)} %bitcast.5, f32[64,112,128]{2,1,0:T(8,128)} %get-tuple-element.6.f_hbm, f32[64,128]{1,0:T(8,128)} %t_ref.3, f32[8,128]{1,0:T(8,128)} %get-tuple-element.7.dt_ref, f32[1,784]{1,0:T(1,128)} %broadcast_in_dim.9.factor_ref, ...), custom_call_target="tpu_custom_call" | custom-call | tf_op jit(solution)/shard_map/burn/pallas_call | solution.py:391
